TPU v7x, 32 devices: a whole 2x2x4 slice. The times are simulated.
32 devices in a mesh: mem: 8 (over y, x, core), lat: 4 (over z).
Axes of the slice: x: 2, y: 2, z: 4, core: 2. Of those that a mesh axis runs over, the one named last changes fastest.
Arguments:
- perturb: bfloat16 [32, 4, 128, 1024], P('mem', None, 'lat'), may hold values from -16 to 16
- gradient: float32 [4, 128, 1024], P(None, 'lat', 'mem'), may hold values from -6 to 6
- k_north: float32 [4, 128, 1024], P(None, 'lat'), may hold values from 0.1 to 0.35
- k_east: float32 [4, 128, 1024], P(None, 'lat'), may hold values from 0.02 to 0.15
- scale: float32 [4, 128, 1024], P(None, 'lat'), may hold values from 0.25 to 1
Outputs:
- product: float32 [4, 128, 1024], P(None, 'lat', 'mem')
All inputs are finite; a program needn't handle non-finite values.
Results may differ from a plain program's by a relative error of at most 0.0003.
Values sent between devices are 32-bit elements; how exact they have to be, the bound alone decides.
A program may use at most 128 MiB of HBM per device.

v0:
```python
import jax
import jax.numpy as jnp
from jax import lax
from jax.sharding import PartitionSpec as P

SWEEP = 4


def with_halo(array, sides, width):
    for axis, dim in sides:
        size, length = (lax.axis_size(axis), array.shape[dim])
        up = [(i, (i + 1) % size) for i in range(size - 1)]
        down = [(j, i) for i, j in up]
        last = lax.slice_in_dim(array, length - width, length, axis=dim)
        leading = lax.slice_in_dim(array, 0, width, axis=dim)
        before = lax.ppermute(last, axis, up)
        after = lax.ppermute(leading, axis, down)
        array = jnp.concatenate([before, array, after], axis=dim)
    return array


def spread(values, k_north, k_east):
    middle = values[..., 1:-1, :]
    north_flux = k_north[:, 1:-1] * (values[..., 2:, :] - middle)
    south_flux = k_north[:, :-2] * (middle - values[..., :-2, :])
    east_face = k_east[:, 1:-1]
    east_flux = east_face * (jnp.roll(middle, -1, -1) - middle) - jnp.roll(east_face, 1, -1) * (
        middle - jnp.roll(middle, 1, -1)
    )
    return north_flux - south_flux + east_flux


def adjoint_step(values, coefficients):
    return values[..., 1:-1, :] + spread(coefficients[2] * values, coefficients[0], coefficients[1])


def forward_step(values, coefficients):
    return values[..., 1:-1, :] + coefficients[2][:, 1:-1] * spread(
        values, coefficients[0], coefficients[1]
    )


def shards(perturb, gradient, k_north, k_east, scale):
    member_count = perturb.shape[0]
    row_count = perturb.shape[2]
    row_start = lax.axis_index("lat") * row_count
    global_rows = row_start + jnp.arange(row_count, dtype=jnp.int32)
    top_row = global_rows == lax.axis_size("lat") * row_count - 1
    masked_north = jnp.where(top_row[None, :, None], jnp.float32(0.0), k_north)
    field = perturb.astype(jnp.float32) * lax.all_gather(gradient, "mem", axis=2, tiled=True)[None]
    halo_depth = SWEEP
    stacked = jnp.stack([masked_north, k_east, scale])
    padded_coef = with_halo(stacked, (("lat", 2),), halo_depth)
    for stepper in (adjoint_step, forward_step):
        values = with_halo(field, (("lat", 2),), SWEEP)
        for section in range(SWEEP):
            row_span = row_count + 2 * (SWEEP - section)
            values = stepper(
                values, lax.slice_in_dim(padded_coef, section, section + row_span, axis=2)
            )
        field = values
    member_terms = jnp.sum(perturb.astype(jnp.float32) * field, axis=0)
    summed = lax.psum_scatter(member_terms, "mem", scatter_dimension=2, tiled=True)
    return summed / jnp.float32(member_count * lax.axis_size("mem") - 1)


def solution(mesh):
    placed = (
        P("mem", None, "lat", None),
        P(None, "lat", "mem"),
        P(None, "lat", None),
        P(None, "lat", None),
        P(None, "lat", None),
    )
    return jax.shard_map(
        shards, mesh=mesh, in_specs=placed, out_specs=P(None, "lat", "mem"), check_vma=False
    )
```

profile of v0, /device:TPU:0, one launch (start us, length us, event | category | flops | bytes accessed | tf_op | source)
XLA Modules:
  0.0 127.1 jit_solution(3644900338413348817)
XLA Ops:
  6.5 1.3 select_bitcast_fusion
  7.8 1.2 pad_maximum_fusion.13
  9.0 4.9 %collective-permute-start.2 = (f32[3,4,4,1024]{3,2,1,0:T(4,128)S(1)}, f32[3,4,4,1024]{3,2,1,0:T(4,128)S(1)}, u32[]{:S(2)}, u32[]{:S(2)}) collective-permute-start(f32[3,4,4,1024]{3,2,1,0:T(4,128)S(1)} %get-tuple-element.59), channel_id=1, source_target_pairs={{0,1},{1,2},{2,3},{4,5},{5,6},{6,7},{8,9},{9,10},{10,11},{12,13},{... | collective-permute-start | bytes 589832 | tf_op jit(solution)/shard_map/ppermute | solution.py:16
  14.0 1.4 %collective-permute-start.3 = (f32[3,4,4,1024]{3,2,1,0:T(4,128)S(1)}, f32[3,4,4,1024]{3,2,1,0:T(4,128)S(1)}, u32[]{:S(2)}, u32[]{:S(2)}) collective-permute-start(f32[3,4,4,1024]{3,2,1,0:T(4,128)S(1)} %get-tuple-element.60), channel_id=1, source_target_pairs={{1,0},{2,1},{3,2},{5,4},{6,5},{7,6},{9,8},{10,9},{11,10},{13,12},{... | collective-permute-start | bytes 589832 | tf_op jit(solution)/shard_map/ppermute | solution.py:17
  15.4 11.0 %all_gather.3 = f32[4,32,1024]{2,1,0:T(8,128)S(1)} all-gather(f32[4,32,128]{2,1,0:T(8,128)S(1)} %copy-done.3), channel_id=1, replica_groups=mesh['mem'=8,'lat'=4] {'mem'}, dimensions={2}, use_global_device_ids=true | all-gather | bytes 589824 | tf_op jit(solution)/shard_map/all_gather | solution.py:50
  26.9 4.6 %collective-permute-start = (f32[4,4,4,1024]{3,2,1,0:T(4,128)S(1)}, f32[4,4,4,1024]{3,2,1,0:T(4,128)S(1)}, u32[]{:S(2)}, u32[]{:S(2)}) collective-permute-start(f32[4,4,4,1024]{3,2,1,0:T(4,128)S(1)} %get-tuple-element.45), channel_id=1, source_target_pairs={{0,1},{1,2},{2,3},{4,5},{5,6},{6,7},{8,9},{9,10},{10,11},{12,13},{... | collective-permute-start | bytes 786440 | tf_op jit(solution)/shard_map/ppermute | solution.py:16
  31.4 1.3 %collective-permute-start.1 = (f32[4,4,4,1024]{3,2,1,0:T(4,128)S(1)}, f32[4,4,4,1024]{3,2,1,0:T(4,128)S(1)}, u32[]{:S(2)}, u32[]{:S(2)}) collective-permute-start(f32[4,4,4,1024]{3,2,1,0:T(4,128)S(1)} %get-tuple-element.46), channel_id=1, source_target_pairs={{1,0},{2,1},{3,2},{5,4},{6,5},{7,6},{9,8},{10,9},{11,10},{13,12},{... | collective-permute-start | bytes 786440 | tf_op jit(solution)/shard_map/ppermute | solution.py:17
  36.4 1.0 collective-permute-done
  37.5 4.1 %collective-permute-done.1 = f32[4,4,4,1024]{3,2,1,0:T(4,128)S(1)} collective-permute-done((f32[4,4,4,1024]{3,2,1,0:T(4,128)S(1)}, f32[4,4,4,1024]{3,2,1,0:T(4,128)S(1)}, u32[]{:S(2)}, u32[]{:S(2)}) %collective-permute-start.1) | collective-permute-done | bytes 262176 | tf_op jit(solution)/shard_map/ppermute | solution.py:17
  41.6 0.8 pad_maximum_fusion.4
  42.4 1.4 %fusion.89 = (f32[4,4,38,1023]{3,2,1,0:T(8,128)S(1)}, f32[4,4,38,1023]{3,2,1,0:T(8,128)S(1)}) fusion(f32[4,4,40,1024]{3,2,1,0:T(8,128)S(1)} %get-tuple-element.38), kind=kLoop, calls=%fused_computation.151 | loop fusion | bytes 9951744 | tf_op jit(solution)/shard_map/jit(_roll_static)/slice | solution.py:27
  44.0 2.7 %broadcast_multiply_fusion.2 = (f32[4,4,38,1024]{3,2,1,0:T(8,128)S(1)}, f32[4,4,38,1024]{3,2,1,0:T(8,128)S(1)}) fusion(f32[4,38,1024]{2,1,0:T(8,128)S(1)} %get-tuple-element.55, f32[4,4,38,1023]{3,2,1,0:T(8,128)S(1)} %get-tuple-element.40, f32[4,4,38,1]{3,2,1,0:T(8,128)S(1)} %get-tuple-element.42, f32[4,38,1024]{2,1,0:T(8,128)S(1)} %pad_maximum_fusion.7, ...), kind=kLoop, calls=%fused_computation.114 | loop fusion | flops 9338880 | bytes 23035904 | tf_op jit(solution)/shard_map/mul | solution.py:34
  46.7 1.4 %fusion.87 = (f32[4,4,36,1023]{3,2,1,0:T(8,128)S(1)}, f32[4,4,36,1023]{3,2,1,0:T(8,128)S(1)}) fusion(f32[4,4,38,1024]{3,2,1,0:T(8,128)S(1)} %get-tuple-element.9), kind=kLoop, calls=%fused_computation.149 | loop fusion | bytes 9427968 | tf_op jit(solution)/shard_map/jit(_roll_static)/slice | solution.py:27
  48.3 2.5 %broadcast_multiply_fusion.1 = (f32[4,4,36,1024]{3,2,1,0:T(8,128)S(1)}, f32[4,4,36,1024]{3,2,1,0:T(8,128)S(1)}) fusion(f32[4,36,1024]{2,1,0:T(8,128)S(1)} %get-tuple-element.52, f32[4,4,36,1023]{3,2,1,0:T(8,128)S(1)} %get-tuple-element.34, f32[4,4,36,1]{3,2,1,0:T(8,128)S(1)} %get-tuple-element.36, f32[4,36,1024]{2,1,0:T(8,128)S(1)} %get-tuple-element.69, ...), kind=kLoop, calls=%fused_computation.113 | loop fusion | flops 8847360 | bytes 21823488 | tf_op jit(solution)/shard_map/mul | solution.py:34
  50.8 1.4 %fusion.85 = (f32[4,4,34,1023]{3,2,1,0:T(8,128)S(1)}, f32[4,4,34,1023]{3,2,1,0:T(8,128)S(1)}) fusion(f32[4,4,36,1024]{3,2,1,0:T(8,128)S(1)} %get-tuple-element.7), kind=kLoop, calls=%fused_computation.147 | loop fusion | bytes 8904192 | tf_op jit(solution)/shard_map/jit(_roll_static)/slice | solution.py:27
  52.4 2.5 %broadcast_multiply_fusion = (f32[4,4,34,1024]{3,2,1,0:T(8,128)S(1)}, f32[4,4,34,1024]{3,2,1,0:T(8,128)S(1)}) fusion(f32[4,34,1024]{2,1,0:T(8,128)S(1)} %get-tuple-element.49, f32[4,4,34,1023]{3,2,1,0:T(8,128)S(1)} %get-tuple-element.30, f32[4,4,34,1]{3,2,1,0:T(8,128)S(1)} %get-tuple-element.32, f32[4,34,1024]{2,1,0:T(8,128)S(1)} %get-tuple-element.70, ...), kind=kLoop, calls=%fused_computation.112 | loop fusion | flops 8355840 | bytes 20611072 | tf_op jit(solution)/shard_map/mul | solution.py:34
  54.9 1.1 fusion.84
  56.2 1.8 %fusion.65 = f32[4,4,32,1024]{3,2,1,0:T(8,128)S(1)} fusion(f32[4,4,34,1024]{3,2,1,0:T(8,128)S(1)} %get-tuple-element.5, f32[4,4,34,1024]{3,2,1,0:T(8,128)S(1)} %get-tuple-element.6, f32[4,4,32,1]{3,2,1,0:T(8,128)S(1)} %get-tuple-element.26, f32[4,4,32,1023]{3,2,1,0:T(8,128)S(1)} %get-tuple-element.28, f32[4,4,32,1023]{3,2,1,0:T(8,128)S(1)} %get-tuple-element.27, ...), kind=kLoop, calls=%fused_computation.98 | loop fusion | flops 7340032 | bytes 16777216 | tf_op jit(solution)/shard_map/add | solution.py:34
  58.1 3.5 %collective-permute-start.4 = (f32[4,4,4,1024]{3,2,1,0:T(4,128)S(1)}, f32[4,4,4,1024]{3,2,1,0:T(4,128)S(1)}, u32[]{:S(2)}, u32[]{:S(2)}) collective-permute-start(f32[4,4,4,1024]{3,2,1,0:T(4,128)S(1)} %get-tuple-element.43), channel_id=1, source_target_pairs={{0,1},{1,2},{2,3},{4,5},{5,6},{6,7},{8,9},{9,10},{10,11},{12,13},{... | collective-permute-start | bytes 786440 | tf_op jit(solution)/shard_map/ppermute | solution.py:16
  61.6 1.3 %collective-permute-start.5 = (f32[4,4,4,1024]{3,2,1,0:T(4,128)S(1)}, f32[4,4,4,1024]{3,2,1,0:T(4,128)S(1)}, u32[]{:S(2)}, u32[]{:S(2)}) collective-permute-start(f32[4,4,4,1024]{3,2,1,0:T(4,128)S(1)} %get-tuple-element.44), channel_id=1, source_target_pairs={{1,0},{2,1},{3,2},{5,4},{6,5},{7,6},{9,8},{10,9},{11,10},{13,12},{... | collective-permute-start | bytes 786440 | tf_op jit(solution)/shard_map/ppermute | solution.py:17
  63.1 3.3 %collective-permute-done.4 = f32[4,4,4,1024]{3,2,1,0:T(4,128)S(1)} collective-permute-done((f32[4,4,4,1024]{3,2,1,0:T(4,128)S(1)}, f32[4,4,4,1024]{3,2,1,0:T(4,128)S(1)}, u32[]{:S(2)}, u32[]{:S(2)}) %collective-permute-start.4) | collective-permute-done | bytes 262176 | tf_op jit(solution)/shard_map/ppermute | solution.py:16
  66.5 4.1 %collective-permute-done.5 = f32[4,4,4,1024]{3,2,1,0:T(4,128)S(1)} collective-permute-done((f32[4,4,4,1024]{3,2,1,0:T(4,128)S(1)}, f32[4,4,4,1024]{3,2,1,0:T(4,128)S(1)}, u32[]{:S(2)}, u32[]{:S(2)}) %collective-permute-start.5) | collective-permute-done | bytes 262176 | tf_op jit(solution)/shard_map/ppermute | solution.py:17
  71.2 1.4 %fusion.82 = (f32[4,4,38,1023]{3,2,1,0:T(8,128)S(1)}, f32[4,4,38,1023]{3,2,1,0:T(8,128)S(1)}) fusion(f32[4,4,40,1024]{3,2,1,0:T(8,128)S(1)} %pad_maximum_fusion.5), kind=kLoop, calls=%fused_computation.144 | loop fusion | bytes 9951744 | tf_op jit(solution)/shard_map/jit(_roll_static)/slice | solution.py:28
  72.6 2.7 %fusion.18 = f32[4,4,38,1024]{3,2,1,0:T(8,128)S(1)} fusion(f32[4,4,4,1024]{3,2,1,0:T(4,128)S(1)} %collective-permute-done.5, f32[4,4,32,1024]{3,2,1,0:T(8,128)S(1)} %fusion.65, f32[4,4,4,1024]{3,2,1,0:T(4,128)S(1)} %collective-permute-done.4, f32[4,4,40,1024]{3,2,1,0:T(8,128)S(1)} %pad_maximum_fusion.5, f32[4,4,38,1023]{3,2,1,0:T(8,128)S(1)} %get-tuple-element.24, ...), kind=kLoop, calls=%fused_computation.25 | loop fusion | flops 11829248 | bytes 20671744 | tf_op jit(solution)/shard_map/add | solution.py:38
  75.3 1.4 %fusion.81 = (f32[4,4,36,1023]{3,2,1,0:T(8,128)S(1)}, f32[4,4,36,1023]{3,2,1,0:T(8,128)S(1)}) fusion(f32[4,4,38,1024]{3,2,1,0:T(8,128)S(1)} %fusion.18), kind=kLoop, calls=%fused_computation.143 | loop fusion | bytes 9427968 | tf_op jit(solution)/shard_map/jit(_roll_static)/slice | solution.py:28
  76.9 2.1 %fusion.10 = f32[4,4,36,1024]{3,2,1,0:T(8,128)S(1)} fusion(f32[4,4,38,1024]{3,2,1,0:T(8,128)S(1)} %fusion.18, f32[4,4,36,1]{3,2,1,0:T(8,128)S(1)} %get-tuple-element.20, f32[4,4,36,1023]{3,2,1,0:T(8,128)S(1)} %get-tuple-element.22, f32[4,4,36,1023]{3,2,1,0:T(8,128)S(1)} %get-tuple-element.21, f32[4,4,36,1]{3,2,1,0:T(8,128)S(1)} %get-tuple-element.19, ...), kind=kLoop, calls=%fused_computation.15 | loop fusion | flops 8847360 | bytes 17104896 | tf_op jit(solution)/shard_map/add | solution.py:38
  79.0 1.2 fusion.79
  80.4 2.0 %fusion.4 = f32[4,4,34,1024]{3,2,1,0:T(8,128)S(1)} fusion(f32[4,4,36,1024]{3,2,1,0:T(8,128)S(1)} %fusion.10, f32[4,4,34,1]{3,2,1,0:T(8,128)S(1)} %get-tuple-element.16, f32[4,4,34,1023]{3,2,1,0:T(8,128)S(1)} %get-tuple-element.18, f32[4,4,34,1023]{3,2,1,0:T(8,128)S(1)} %get-tuple-element.17, f32[4,4,34,1]{3,2,1,0:T(8,128)S(1)} %get-tuple-element.15, ...), kind=kLoop, calls=%fused_computation.7 | loop fusion | flops 8355840 | bytes 16154624 | tf_op jit(solution)/shard_map/add | solution.py:38
  82.4 1.1 fusion.77
  83.7 2.7 %fusion.55 = f32[4,32,1024]{2,1,0:T(8,128)} fusion(bf16[4,4,32,1024]{3,2,1,0:T(8,128)(2,1)S(1)} %copy-done, f32[4,4,34,1024]{3,2,1,0:T(8,128)S(1)} %fusion.4, f32[4,4,32,1]{3,2,1,0:T(8,128)S(1)} %get-tuple-element.12, f32[4,4,32,1023]{3,2,1,0:T(8,128)S(1)} %get-tuple-element.14, f32[4,4,32,1023]{3,2,1,0:T(8,128)S(1)} %get-tuple-element.13, ...), kind=kLoop, calls=%fused_computation.85 | loop fusion | flops 9306112 | bytes 14680064 | tf_op jit(solution)/shard_map/reduce_sum | solution.py:62
  86.4 32.4 %reduce-scatter.2.cloned.1.call-done = f32[4,32,128]{2,1,0:T(8,128)} async-done(((f32[4,32,1024]{2,1,0:T(8,128)}), f32[4,32,128]{2,1,0:T(8,128)}) %reduce-scatter.2.cloned.1.call-update) | async-done | bytes 65552 | tf_op jit(solution)/shard_map/reduce_scatter | solution.py:63
  118.8 1.5 %broadcast_multiply_fusion.4 = f32[4,32,128]{2,1,0:T(8,128)} fusion(f32[4,32,128]{2,1,0:T(8,128)} %reduce-scatter.2.cloned.1.call-done), kind=kLoop, calls=%fused_computation.136 | loop fusion | flops 16384 | bytes 131072 | tf_op jit(solution)/shard_map/div | solution.py:64
  (50 shorter events, 6.0 us)
Async XLA Ops:
  6.5 8.9 %copy-start.3 = (f32[4,32,128]{2,1,0:T(8,128)S(1)}, f32[4,32,128]{2,1,0:T(8,128)}, u32[]{:S(2)}) copy-start(f32[4,32,128]{2,1,0:T(8,128)} %param.6) | copy-start | bytes 196612
  6.5 19.9 %copy-start = (bf16[4,4,32,1024]{3,2,1,0:T(8,128)(2,1)S(1)}, bf16[4,4,32,1024]{3,2,1,0:T(8,128)(2,1)}, u32[]{:S(2)}) copy-start(bf16[4,4,32,1024]{3,2,1,0:T(8,128)(2,1)} %param.5) | copy-start | bytes 3145732
  6.5 112.3 %reduce-scatter.2.cloned.1.call-start = ((), (), s32[]{:S(2)}) async-start(), calls=%async_computation.1 | async-start | bytes 589824 | tf_op jit(solution)/shard_map/reduce_scatter | solution.py:63
  9.0 23.7 %collective-permute-start.2 = (f32[3,4,4,1024]{3,2,1,0:T(4,128)S(1)}, f32[3,4,4,1024]{3,2,1,0:T(4,128)S(1)}, u32[]{:S(2)}, u32[]{:S(2)}) collective-permute-start(f32[3,4,4,1024]{3,2,1,0:T(4,128)S(1)} %get-tuple-element.59), channel_id=1, source_target_pairs={{0,1},{1,2},{2,3},{4,5},{5,6},{6,7},{8,9},{9,10},{10,11},{12,13},{... | collective-permute-start | bytes 589832 | tf_op jit(solution)/shard_map/ppermute | solution.py:16
  14.0 18.8 %copy-start.1 = (f32[4,32,1024]{2,1,0:T(8,128)S(1)}, f32[4,32,1024]{2,1,0:T(8,128)}, u32[]{:S(2)}) copy-start(f32[4,32,1024]{2,1,0:T(8,128)} %param.9) | copy-start | bytes 1572868
  14.0 18.8 %copy-start.2 = (f32[4,32,1024]{2,1,0:T(8,128)S(1)}, f32[4,32,1024]{2,1,0:T(8,128)}, u32[]{:S(2)}) copy-start(f32[4,32,1024]{2,1,0:T(8,128)} %param.8) | copy-start | bytes 1572868
  14.0 18.8 %collective-permute-start.3 = (f32[3,4,4,1024]{3,2,1,0:T(4,128)S(1)}, f32[3,4,4,1024]{3,2,1,0:T(4,128)S(1)}, u32[]{:S(2)}, u32[]{:S(2)}) collective-permute-start(f32[3,4,4,1024]{3,2,1,0:T(4,128)S(1)} %get-tuple-element.60), channel_id=1, source_target_pairs={{1,0},{2,1},{3,2},{5,4},{6,5},{7,6},{9,8},{10,9},{11,10},{13,12},{... | collective-permute-start | bytes 589832 | tf_op jit(solution)/shard_map/ppermute | solution.py:17
  26.9 10.6 %collective-permute-start = (f32[4,4,4,1024]{3,2,1,0:T(4,128)S(1)}, f32[4,4,4,1024]{3,2,1,0:T(4,128)S(1)}, u32[]{:S(2)}, u32[]{:S(2)}) collective-permute-start(f32[4,4,4,1024]{3,2,1,0:T(4,128)S(1)} %get-tuple-element.45), channel_id=1, source_target_pairs={{0,1},{1,2},{2,3},{4,5},{5,6},{6,7},{8,9},{9,10},{10,11},{12,13},{... | collective-permute-start | bytes 786440 | tf_op jit(solution)/shard_map/ppermute | solution.py:16
  31.4 10.2 %collective-permute-start.1 = (f32[4,4,4,1024]{3,2,1,0:T(4,128)S(1)}, f32[4,4,4,1024]{3,2,1,0:T(4,128)S(1)}, u32[]{:S(2)}, u32[]{:S(2)}) collective-permute-start(f32[4,4,4,1024]{3,2,1,0:T(4,128)S(1)} %get-tuple-element.46), channel_id=1, source_target_pairs={{1,0},{2,1},{3,2},{5,4},{6,5},{7,6},{9,8},{10,9},{11,10},{13,12},{... | collective-permute-start | bytes 786440 | tf_op jit(solution)/shard_map/ppermute | solution.py:17
  58.1 8.4 %collective-permute-start.4 = (f32[4,4,4,1024]{3,2,1,0:T(4,128)S(1)}, f32[4,4,4,1024]{3,2,1,0:T(4,128)S(1)}, u32[]{:S(2)}, u32[]{:S(2)}) collective-permute-start(f32[4,4,4,1024]{3,2,1,0:T(4,128)S(1)} %get-tuple-element.43), channel_id=1, source_target_pairs={{0,1},{1,2},{2,3},{4,5},{5,6},{6,7},{8,9},{9,10},{10,11},{12,13},{... | collective-permute-start | bytes 786440 | tf_op jit(solution)/shard_map/ppermute | solution.py:16
  61.6 9.1 %collective-permute-start.5 = (f32[4,4,4,1024]{3,2,1,0:T(4,128)S(1)}, f32[4,4,4,1024]{3,2,1,0:T(4,128)S(1)}, u32[]{:S(2)}, u32[]{:S(2)}) collective-permute-start(f32[4,4,4,1024]{3,2,1,0:T(4,128)S(1)} %get-tuple-element.44), channel_id=1, source_target_pairs={{1,0},{2,1},{3,2},{5,4},{6,5},{7,6},{9,8},{10,9},{11,10},{13,12},{... | collective-permute-start | bytes 786440 | tf_op jit(solution)/shard_map/ppermute | solution.py:17
Sparse Core Ops, SparseCore 0:
  86.5 32.2 reduce-scatter.1
where the time goes:
time: 127 us
  waiting for transfers between devices  45.1 us (36%)
  other arithmetic  25.9 us (20%)
  starting transfers between devices  17 us (13%)
  local copies, waits for them, and re-layouts  14.2 us (11%)
  between operations  13.9 us (11%)
  blocking collectives  11 us (9%)
    reduce_scatter x1, waiting for transfers between devices, shards(): lax.psum_scatter(member_terms, 'mem', scatter_dimension=2, tiled=True)  32.4 us
    ppermute x3, starting transfers between devices, with_halo(): before = lax.ppermute(last, axis, up)  13 us
    all_gather x1, blocking collectives, shards(): lax.all_gather(gradient, 'mem', axis=2, tiled=True)[None]  11 us
    ppermute x3, waiting for transfers between devices, with_halo(): after = lax.ppermute(leading, axis, down)  8.26 us
    mul x3, other arithmetic, adjoint_step(): coefficients[2] * values  7.71 us
    slice x9, local copies, waits for them, and re-layouts, spread(): jnp.roll(middle, 1, -1)  6.88 us
    add x3, other arithmetic, forward_step(): values[..., 1:-1, :]  6.72 us
    slice x6, local copies, waits for them, and re-layouts, spread(): jnp.roll(middle, -1, -1) - middle  4.74 us
  transfers between devices with their start and end apart: 7, of which 5 were waited for; matrix products, arithmetic and copies ran while one was open for 3% of the time, Pallas kernels for 0%

commit v1 on v0

v1 whole, which is shorter than its diff:
```python
import functools

import jax
import jax.numpy as jnp
from jax import lax
from jax.experimental import pallas as pl
from jax.experimental.pallas import tpu as pltpu
from jax.sharding import PartitionSpec as P

SWEEP = 4
H = SWEEP


def twice(x):
    return jnp.concatenate([x, x], axis=-2)


def sweep_kernel(
    n, nz, fused, p_ref, g_ref, kn_ref, ke_ref, s_ref, out_ref,
    pt, kt, co, rs, ua, ub, uc, ud, gs, gall, part, rpart,
    ksend, krecv, usend, urecv, csend, crecv, gsend, grecv, psend, precv,
):
    members, levels, rows, lon = p_ref.shape
    groups = members // 2
    me = lax.axis_index("mem")
    z = lax.axis_index("lat")
    low, high = z > 0, z < nz - 1
    total = n * members
    width = gs.shape[-1]

    barrier = pltpu.get_barrier_semaphore()
    if fused:
        for d in range(1, n):
            pl.semaphore_signal(
                barrier, inc=1, device_id={"mem": lax.rem(me + d, n)},
                device_id_type=pl.DeviceIdType.MESH)

    @pl.when(low)
    def _():
        pl.semaphore_signal(barrier, inc=1, device_id={"lat": z - 1},
                            device_id_type=pl.DeviceIdType.MESH)

    @pl.when(high)
    def _():
        pl.semaphore_signal(barrier, inc=1, device_id={"lat": z + 1},
                            device_id_type=pl.DeviceIdType.MESH)

    gs[...] = jnp.swapaxes(g_ref[...], 0, 1)
    keep = jnp.logical_or(
        lax.broadcasted_iota(jnp.int32, (levels, rows, lon), 1) < rows - 1, high)
    kt[0, pl.ds(H, rows)] = jnp.swapaxes(jnp.where(keep, kn_ref[...], 0.0), 0, 1)
    kt[1, pl.ds(H, rows)] = jnp.swapaxes(ke_ref[...], 0, 1)
    kt[2, pl.ds(H, rows)] = jnp.swapaxes(s_ref[...], 0, 1)

    peers = (n - 1 if fused else 0) + low.astype(jnp.int32) + high.astype(jnp.int32)
    pl.semaphore_wait(barrier, peers)

    def halo(buf, sends, recvs, lead):
        at = lambda first: buf.at[:, pl.ds(first, H)] if lead else buf.at[pl.ds(first, H)]
        down = pltpu.make_async_remote_copy(
            src_ref=at(H), dst_ref=at(H + rows), send_sem=sends.at[0],
            recv_sem=recvs.at[0], device_id={"lat": z - 1},
            device_id_type=pl.DeviceIdType.MESH)
        up = pltpu.make_async_remote_copy(
            src_ref=at(rows), dst_ref=at(0), send_sem=sends.at[1],
            recv_sem=recvs.at[1], device_id={"lat": z + 1},
            device_id_type=pl.DeviceIdType.MESH)
        return down, up

    def start_halo(pair):
        pl.when(low)(pair[0].start)
        pl.when(high)(pair[1].start)

    def wait_sent(pair):
        pl.when(low)(pair[0].wait_send)
        pl.when(high)(pair[1].wait_send)

    khalo = halo(kt, ksend, krecv, True)
    uhalo = halo(ua, usend, urecv, False)
    chalo = halo(uc, csend, crecv, False)

    gcopies = []
    if fused:
        for d in range(1, n):
            peer = lax.rem(me + d, n)
            c = pltpu.make_async_remote_copy(
                src_ref=gs, dst_ref=gall.at[me], send_sem=gsend.at[d],
                recv_sem=grecv.at[d], device_id={"mem": peer},
                device_id_type=pl.DeviceIdType.MESH)
            c.start()
            gcopies.append(c)
        gall[me] = gs[...]
    start_halo(khalo)

    def blank(first):
        kt[0:2, first:first + H] = jnp.zeros((2, H, levels, lon), jnp.float32)
        kt[2, first:first + H] = jnp.ones((H, levels, lon), jnp.float32)
        ua[first:first + H] = jnp.zeros((H,) + ua.shape[1:], jnp.float32)
        uc[first:first + H] = jnp.zeros((H,) + uc.shape[1:], jnp.float32)

    pl.when(jnp.logical_not(low))(lambda: blank(0))
    pl.when(jnp.logical_not(high))(lambda: blank(H + rows))

    for half in range(rows // 16):
        block = p_ref[:, :, half * 16:(half + 1) * 16, :].astype(jnp.float32)
        block = block.reshape(members * levels, 16, lon)
        pt[half * 16:(half + 1) * 16] = jnp.swapaxes(block, 0, 1)

    def coefficient_row(r):
        kn, south = twice(kt[0, r]), twice(kt[0, r - 1])
        ke, s = twice(kt[1, r]), twice(kt[2, r])
        west = pltpu.roll(ke, 1, 1)
        co[0, r] = 1.0 - s * (kn + south + ke + west)
        co[1, r] = s * kn
        co[2, r] = s * south
        co[3, r] = s * ke
        co[4, r] = s * west
        rs[r] = 1.0 / s

    def each_row(first, last, body, block=4):
        count = last - first
        full = count // block

        def many(i, carry):
            for b in range(block):
                body(first + i * block + b)
            return carry

        if full:
            lax.fori_loop(0, full, many, 0)
        for r in range(first + full * block, last):
            body(r)

    each_row(H + 1, H + rows, coefficient_row)

    for c in gcopies:
        c.wait_recv()

    def start_row(r):
        if fused:
            g = jnp.concatenate([gall[b, r - H] for b in range(n)], axis=-1)
        else:
            g = gs[r - H]
        sg = twice(g * kt[2, r])
        for q in range(groups):
            ua[r, 8 * q:8 * q + 8] = pt[r - H, 8 * q:8 * q + 8] * sg

    each_row(H, 2 * H, start_row)
    each_row(rows, rows + H, start_row)
    start_halo(uhalo)
    each_row(2 * H, rows, start_row)

    def stepped(src, r):
        c0, cn, cs, ce, cw = (co[i, r] for i in range(5))
        result = []
        for q in range(groups):
            part_of = pl.ds(8 * q, 8)
            u = src[r, part_of]
            result.append(
                c0 * u + (cn * src[r + 1, part_of] + cs * src[r - 1, part_of])
                + (ce * pltpu.roll(u, lon - 1, 1) + cw * pltpu.roll(u, 1, 1)))
        return result

    def plain(src, dst, r):
        for q, v in enumerate(stepped(src, r)):
            dst[r, 8 * q:8 * q + 8] = v

    def unscaled(src, dst, r):
        inverse = rs[r]
        for q, v in enumerate(stepped(src, r)):
            dst[r, 8 * q:8 * q + 8] = v * inverse

    def product(src, dst, r):
        t = None
        for q, v in enumerate(stepped(src, r)):
            term = v * pt[r - H, 8 * q:8 * q + 8]
            t = term if t is None else t + term
        t = t[:levels] + t[levels:]
        if fused:
            for b in range(n):
                part[b, r - H] = t[:, b * width:(b + 1) * width]
        else:
            part[0, r - H] = t

    chain = [ub, ud] * SWEEP
    first_sweep, second_sweep = [], []
    for k in range(SWEEP):
        last = k == SWEEP - 1
        before = chain[k - 1]
        first_sweep.append(
            (ua if k == 0 else before, uc if last else chain[k], unscaled if last else plain))
        second_sweep.append(
            (uc if k == 0 else before, None if last else chain[k], product if last else plain))

    def inner(sweep):
        for k, (src, dst, fn) in enumerate(sweep):
            each_row(H + k + 1, H + rows - k - 1, functools.partial(fn, src, dst))

    def edge(sweep, upper):
        for k, (src, dst, fn) in enumerate(sweep):
            first = (rows + H - k - 1) if upper else k + 1
            each_row(first, first + H, functools.partial(fn, src, dst))

    inner(first_sweep)

    pl.when(high)(khalo[0].wait_recv)
    pl.when(low)(khalo[1].wait_recv)
    each_row(1, H + 1, coefficient_row)
    each_row(H + rows, H + rows + H - 1, coefficient_row)
    pl.when(high)(uhalo[0].wait_recv)
    pl.when(low)(uhalo[1].wait_recv)
    edge(first_sweep, False)
    pl.when(low)(chalo[0].start)
    edge(first_sweep, True)
    pl.when(high)(chalo[1].start)

    spans = ((H, rows - 2 * H), (0, H), (rows - H, H))
    pcopies = []

    def send_part(i):
        if not fused:
            return
        at, count = spans[i]
        for d in range(1, n):
            peer = lax.rem(me + d, n)
            c = pltpu.make_async_remote_copy(
                src_ref=part.at[peer, pl.ds(at, count)],
                dst_ref=rpart.at[d, pl.ds(at, count)],
                send_sem=psend.at[d, i], recv_sem=precv.at[d, i],
                device_id={"mem": peer}, device_id_type=pl.DeviceIdType.MESH)
            c.start()
            pcopies.append(c)

    inner(second_sweep)
    send_part(0)
    pl.when(low)(chalo[1].wait_recv)
    edge(second_sweep, False)
    send_part(1)
    pl.when(high)(chalo[0].wait_recv)
    edge(second_sweep, True)
    send_part(2)

    if fused:
        for c in pcopies:
            c.wait_recv()
        acc = part[me]
        for d in range(1, n):
            acc = acc + rpart[d]
        out_ref[...] = jnp.swapaxes(acc, 0, 1) / jnp.float32(total - 1)
    else:
        out_ref[...] = jnp.swapaxes(part[0], 0, 1) / jnp.float32(total - 1)

    for pair in (khalo, uhalo, chalo):
        wait_sent(pair)
    for c in gcopies:
        c.wait_send()
    for c in pcopies:
        c.wait_send()


def shards(n, nz, perturb, gradient, k_north, k_east, scale):
    members, levels, rows, lon = perturb.shape
    block = gradient.shape[2]
    fused = block % 128 == 0
    if not fused:
        gradient = lax.all_gather(gradient, "mem", axis=2, tiled=True)
    width = gradient.shape[2]
    units = members * levels
    f32 = jnp.float32
    blocks = n if fused else 1
    vmem = pl.BlockSpec(memory_space=pltpu.VMEM)
    out = pl.pallas_call(
        functools.partial(sweep_kernel, n, nz, fused),
        out_shape=jax.ShapeDtypeStruct((levels, rows, width), f32),
        in_specs=[vmem] * 5,
        out_specs=vmem,
        scratch_shapes=[
            pltpu.VMEM((rows, units, lon), f32),
            pltpu.VMEM((3, rows + 2 * H, levels, lon), f32),
            pltpu.VMEM((5, rows + 2 * H, 2 * levels, lon), f32),
            pltpu.VMEM((rows + 2 * H, 2 * levels, lon), f32),
            pltpu.VMEM((rows + 2 * H, units, lon), f32),
            pltpu.VMEM((rows + 2 * H, units, lon), f32),
            pltpu.VMEM((rows + 2 * H, units, lon), f32),
            pltpu.VMEM((rows + 2 * H, units, lon), f32),
            pltpu.VMEM((rows, levels, width), f32),
            pltpu.VMEM((blocks, rows, levels, width), f32),
            pltpu.VMEM((blocks, rows, levels, width), f32),
            pltpu.VMEM((blocks, rows, levels, width), f32),
            pltpu.SemaphoreType.DMA((2,)),
            pltpu.SemaphoreType.DMA((2,)),
            pltpu.SemaphoreType.DMA((2,)),
            pltpu.SemaphoreType.DMA((2,)),
            pltpu.SemaphoreType.DMA((2,)),
            pltpu.SemaphoreType.DMA((2,)),
            pltpu.SemaphoreType.DMA((n,)),
            pltpu.SemaphoreType.DMA((n,)),
            pltpu.SemaphoreType.DMA((n, 3)),
            pltpu.SemaphoreType.DMA((n, 3)),
        ],
        compiler_params=pltpu.CompilerParams(
            collective_id=0, has_side_effects=True, vmem_limit_bytes=48 * 1024 * 1024),
    )(perturb, gradient, k_north, k_east, scale)
    if not fused:
        out = lax.psum_scatter(out, "mem", scatter_dimension=2, tiled=True)
    return out


def solution(mesh):
    placed = (
        P("mem", None, "lat", None),
        P(None, "lat", "mem"),
        P(None, "lat", None),
        P(None, "lat", None),
        P(None, "lat", None),
    )
    return jax.shard_map(
        functools.partial(shards, mesh.shape["mem"], mesh.shape["lat"]),
        mesh=mesh, in_specs=placed, out_specs=P(None, "lat", "mem"), check_vma=False)
```

time: 127 us -> 41.4 us (0.33)
  waiting for transfers between devices: 45.1 us -> 0 us
  Pallas kernels: 0 us -> 35.3 us
  other arithmetic: 25.9 us -> 0 us
  starting transfers between devices: 17 us -> 0 us
  between operations: 13.9 us -> 0.01 us
  blocking collectives: 11 us -> 0 us
  local copies, waits for them, and re-layouts: 14.2 us -> 5.82 us
    pallas_call x0 -> x1, Pallas kernels: none -> 35.3 us  [shards(): pl.pallas_call(functools.partial(sweep_kernel, n, nz, fused), out_shape=j...]
    reduce_scatter x1 -> x0, waiting for transfers between devices: 32.4 us -> none  [shards(): lax.psum_scatter(member_terms, 'mem', scatter_dimension=2, tiled=True)]
    ppermute x6 -> x0, starting transfers between devices: 17 us -> none  [the longest x3 13 us: with_halo(): before = lax.ppermute(last, axis, up)]
    slice x34 -> x0, local copies, waits for them, and re-layouts: 13.1 us -> none  [the longest x9 6.88 us: spread(): jnp.roll(middle, 1, -1)]
    ppermute x6 -> x0, waiting for transfers between devices: 12.6 us -> none  [the longest x3 8.26 us: with_halo(): after = lax.ppermute(leading, axis, down)]
    all_gather x1 -> x0, blocking collectives: 11 us -> none  [shards(): lax.all_gather(gradient, 'mem', axis=2, tiled=True)[None]]
    add x4 -> x0, other arithmetic: 8.53 us -> none  [the longest x3 6.72 us: forward_step(): values[..., 1:-1, :]]
    mul x4 -> x0, other arithmetic: 8.01 us -> none  [the longest x3 7.71 us: adjoint_step(): coefficients[2] * values]
  transfers between devices with their start and end apart: 7 -> 0, of which waited for: 5 -> 0; matrix products, arithmetic and copies ran while one was open for 3% -> 0% of each run, Pallas kernels for 0% -> 0%
where the time goes in v1:
time: 41.4 us; the launch traced here: 41.1 us
  Pallas kernels  35.3 us (85%)
  local copies, waits for them, and re-layouts  5.82 us (14%)
    pallas_call x1, Pallas kernels, shards(): pl.pallas_call(functools.partial(sweep_kernel, n, nz, fused), out_shape=j...  35.3 us
    unnamed x11, local copies, waits for them, and re-layouts  5.82 us

profile of v1, /device:TPU:0, one launch (start us, length us, event | category | flops | bytes accessed | tf_op | source)
XLA Modules:
  0.0 41.1 jit_solution(13638570553852673779)
XLA Ops:
  0.0 0.0 copy-start
  0.0 1.2 %copy-done = bf16[4,4,32,1024]{3,2,1,0:T(8,128)(2,1)S(1)} copy-done((bf16[4,4,32,1024]{3,2,1,0:T(8,128)(2,1)S(1)}, bf16[4,4,32,1024]{3,2,1,0:T(8,128)(2,1)}, u32[]{:S(2)}) %copy-start) | copy-done | bytes 1048600
  1.2 0.0 copy-start.1
  1.2 1.0 %copy-done.1 = f32[4,32,1024]{2,1,0:T(8,128)S(1)} copy-done((f32[4,32,1024]{2,1,0:T(8,128)S(1)}, f32[4,32,1024]{2,1,0:T(8,128)}, u32[]{:S(2)}) %copy-start.1) | copy-done | bytes 524312
  2.3 0.0 copy-start.2
  2.3 1.0 %copy-done.2 = f32[4,32,1024]{2,1,0:T(8,128)S(1)} copy-done((f32[4,32,1024]{2,1,0:T(8,128)S(1)}, f32[4,32,1024]{2,1,0:T(8,128)}, u32[]{:S(2)}) %copy-start.2) | copy-done | bytes 524312
  3.3 0.0 copy-start.3
  3.3 1.0 %copy-done.3 = f32[4,32,1024]{2,1,0:T(8,128)S(1)} copy-done((f32[4,32,1024]{2,1,0:T(8,128)S(1)}, f32[4,32,1024]{2,1,0:T(8,128)}, u32[]{:S(2)}) %copy-start.3) | copy-done | bytes 524312
  4.4 0.0 copy-start.4
  4.4 0.8 %copy-done.4 = f32[4,32,128]{2,1,0:T(8,128)S(1)} copy-done((f32[4,32,128]{2,1,0:T(8,128)S(1)}, f32[4,32,128]{2,1,0:T(8,128)}, u32[]{:S(2)}) %copy-start.4) | copy-done | bytes 65560
  5.2 35.3 %shard_map.55 = f32[4,32,128]{2,1,0:T(8,128)S(1)} custom-call(bf16[4,4,32,1024]{3,2,1,0:T(8,128)(2,1)S(1)} %copy-done, f32[4,32,128]{2,1,0:T(8,128)S(1)} %copy-done.4, f32[4,32,1024]{2,1,0:T(8,128)S(1)} %copy-done.1, f32[4,32,1024]{2,1,0:T(8,128)S(1)} %copy-done.2, f32[4,32,1024]{2,1,0:T(8,128)S(1)} %copy-done.3), custom_call_target="tpu_custom_call" | custom-call | tf_op jit(solution)/shard_map/pallas_call | solution.py:272
  40.5 0.6 %copy.7 = f32[4,32,128]{2,1,0:T(8,128)} copy(f32[4,32,128]{2,1,0:T(8,128)S(1)} %shard_map.55) | data formatting | bytes 131072
Async XLA Ops:
  0.0 1.2 %copy-start = (bf16[4,4,32,1024]{3,2,1,0:T(8,128)(2,1)S(1)}, bf16[4,4,32,1024]{3,2,1,0:T(8,128)(2,1)}, u32[]{:S(2)}) copy-start(bf16[4,4,32,1024]{3,2,1,0:T(8,128)(2,1)} %p_ref.1) | copy-start | bytes 3145732
  1.2 1.0 %copy-start.1 = (f32[4,32,1024]{2,1,0:T(8,128)S(1)}, f32[4,32,1024]{2,1,0:T(8,128)}, u32[]{:S(2)}) copy-start(f32[4,32,1024]{2,1,0:T(8,128)} %kn_ref.1) | copy-start | bytes 1572868
  2.3 1.0 %copy-start.2 = (f32[4,32,1024]{2,1,0:T(8,128)S(1)}, f32[4,32,1024]{2,1,0:T(8,128)}, u32[]{:S(2)}) copy-start(f32[4,32,1024]{2,1,0:T(8,128)} %ke_ref.1) | copy-start | bytes 1572868
  3.3 1.0 %copy-start.3 = (f32[4,32,1024]{2,1,0:T(8,128)S(1)}, f32[4,32,1024]{2,1,0:T(8,128)}, u32[]{:S(2)}) copy-start(f32[4,32,1024]{2,1,0:T(8,128)} %s_ref.1) | copy-start | bytes 1572868
  4.4 0.8 %copy-start.4 = (f32[4,32,128]{2,1,0:T(8,128)S(1)}, f32[4,32,128]{2,1,0:T(8,128)}, u32[]{:S(2)}) copy-start(f32[4,32,128]{2,1,0:T(8,128)} %g_ref.1) | copy-start | bytes 196612

commit v2 on v1

v2 whole, which is shorter than its diff:
```python
import functools

import jax
import jax.numpy as jnp
from jax import lax
from jax.experimental import pallas as pl
from jax.experimental.pallas import tpu as pltpu
from jax.sharding import PartitionSpec as P

SWEEP = 4
H = SWEEP


def twice(x):
    return jnp.concatenate([x, x], axis=-2)


def shuffled(x, order, dims):
    total = None
    for _ in range(2):
        piece = x.astype(jnp.bfloat16)
        moved = lax.dot_general(piece, order, (dims, ((), ())),
                                preferred_element_type=jnp.float32)
        total = moved if total is None else total + moved
        x = x - piece.astype(jnp.float32)
    return total


def sweep_kernel(
    n, nz, fused, p_ref, g_ref, kn_ref, ke_ref, s_ref, out_ref,
    pt, kt, co, rs, ua, ub, uc, ud, order, gp, sums, gs, gall, part, spart, comb, rpart,
    ksend, krecv, usend, urecv, csend, crecv, gsend, grecv, psend, precv,
):
    members, levels, rows, lon = p_ref.shape
    groups = members // 2
    me = lax.axis_index("mem")
    z = lax.axis_index("lat")
    low, high = z > 0, z < nz - 1
    total = n * members
    width = gs.shape[-1]

    barrier = pltpu.get_barrier_semaphore()
    if fused:
        for d in range(1, n):
            pl.semaphore_signal(
                barrier, inc=1, device_id={"mem": lax.rem(me + d, n)},
                device_id_type=pl.DeviceIdType.MESH)

    @pl.when(low)
    def _():
        pl.semaphore_signal(barrier, inc=1, device_id={"lat": z - 1},
                            device_id_type=pl.DeviceIdType.MESH)

    @pl.when(high)
    def _():
        pl.semaphore_signal(barrier, inc=1, device_id={"lat": z + 1},
                            device_id_type=pl.DeviceIdType.MESH)

    chunks = lon // 128

    offset = (lax.broadcasted_iota(jnp.int32, (128, 128), 0)
              - chunks * lax.broadcasted_iota(jnp.int32, (128, 128), 1))

    def order_rows(i, carry):
        row = pl.ds(pl.multiple_of(i * 128, 128), 128)
        for c in range(chunks):
            order[row, c * 128:c * 128 + 128] = jnp.where(
                offset == c - i * 128, 1.0, 0.0).astype(jnp.bfloat16)
        return carry

    gs[...] = jnp.swapaxes(g_ref[...], 0, 1)
    lax.fori_loop(0, chunks, order_rows, 0)

    def east(x):
        return jnp.concatenate([x[:, 128:], pltpu.roll(x[:, :128], 127, 1)], axis=1)

    def west_of(x):
        return jnp.concatenate([pltpu.roll(x[:, lon - 128:], 1, 1), x[:, :lon - 128]], axis=1)

    block = p_ref[...].reshape(members * levels * rows, lon)
    block = jnp.dot(block, order[...], preferred_element_type=jnp.float32)
    pt[...] = jnp.swapaxes(block.reshape(members * levels, rows, lon), 0, 1)

    peers = (n - 1 if fused else 0) + low.astype(jnp.int32) + high.astype(jnp.int32)
    pl.semaphore_wait(barrier, peers)

    def halo(at, sends, recvs, q):
        down = pltpu.make_async_remote_copy(
            src_ref=at(H), dst_ref=at(H + rows), send_sem=sends.at[0, q],
            recv_sem=recvs.at[0, q], device_id={"lat": z - 1},
            device_id_type=pl.DeviceIdType.MESH)
        up = pltpu.make_async_remote_copy(
            src_ref=at(rows), dst_ref=at(0), send_sem=sends.at[1, q],
            recv_sem=recvs.at[1, q], device_id={"lat": z + 1},
            device_id_type=pl.DeviceIdType.MESH)
        return down, up

    def start_halo(pair):
        pl.when(low)(pair[0].start)
        pl.when(high)(pair[1].start)

    def wait_halo(pair):
        pl.when(high)(pair[0].wait_recv)
        pl.when(low)(pair[1].wait_recv)

    def wait_sent(pair):
        pl.when(low)(pair[0].wait_send)
        pl.when(high)(pair[1].wait_send)

    def unit_rows(buf, q):
        return lambda first: buf.at[pl.ds(first, H), pl.ds(8 * q, 8)]

    khalo = halo(lambda first: kt.at[:, pl.ds(first, H)], ksend, krecv, 0)
    uhalo = [halo(unit_rows(ua, q), usend, urecv, q) for q in range(groups)]
    chalo = [halo(unit_rows(uc, q), csend, crecv, q) for q in range(groups)]

    chips, chip, core = n // 2, me // 2, lax.rem(me, 2)
    sibling = 2 * chip + 1 - core

    def remote(src, dst, ssem, rsem, mem):
        return pltpu.make_async_remote_copy(
            src_ref=src, dst_ref=dst, send_sem=ssem, recv_sem=rsem,
            device_id={"mem": mem}, device_id_type=pl.DeviceIdType.MESH)

    def chip_at(d):
        return lax.rem(chip + d, chips)

    gcopies, forwards = [], []
    if fused:
        for d in range(1, chips):
            gcopies.append(remote(gs, gall.at[me], gsend.at[d], grecv.at[d],
                                  2 * chip_at(d) + core))
        forwards.append(remote(gs, gall.at[me], gsend.at[0], grecv.at[0], sibling))
        for c in gcopies + forwards:
            c.start()
        gall[me] = gs[...]

    keep = jnp.logical_or(
        lax.broadcasted_iota(jnp.int32, (levels, rows, lon), 1) < rows - 1, high)
    three = jnp.concatenate(
        [jnp.where(keep, kn_ref[...], 0.0), ke_ref[...], s_ref[...]], axis=0)
    three = shuffled(three.reshape(3 * levels * rows, lon), order[...], ((1,), (0,)))
    three = three.reshape(3, levels, rows, lon)
    for i in range(3):
        kt[i, pl.ds(H, rows)] = jnp.swapaxes(three[i], 0, 1)
    start_halo(khalo)
    for d, c in enumerate(gcopies, 1):
        c.wait_recv()
        at = gall.at[2 * chip_at(chips - d) + core]
        c = remote(at, at, gsend.at[chips + d], grecv.at[chips + d], sibling)
        c.start()
        forwards.append(c)

    def blank(first):
        kt[0:2, first:first + H] = jnp.zeros((2, H, levels, lon), jnp.float32)
        kt[2, first:first + H] = jnp.ones((H, levels, lon), jnp.float32)
        ua[first:first + H] = jnp.zeros((H,) + ua.shape[1:], jnp.float32)
        uc[first:first + H] = jnp.zeros((H,) + uc.shape[1:], jnp.float32)

    pl.when(jnp.logical_not(low))(lambda: blank(0))
    pl.when(jnp.logical_not(high))(lambda: blank(H + rows))

    def coefficient_row(r):
        kn, south = twice(kt[0, r]), twice(kt[0, r - 1])
        ke, s = twice(kt[1, r]), twice(kt[2, r])
        west = west_of(ke)
        co[0, r] = 1.0 - s * (kn + south + ke + west)
        co[1, r] = s * kn
        co[2, r] = s * south
        co[3, r] = s * ke
        co[4, r] = s * west
        rs[r] = 1.0 / s

    def each_row(first, last, body, block=4):
        count = last - first
        full = count // block

        def many(i, carry):
            for b in range(block):
                body(first + i * block + b)
            return carry

        if full:
            lax.fori_loop(0, full, many, 0)
        for r in range(first + full * block, last):
            body(r)

    each_row(H + 1, H + rows, coefficient_row)

    for c in forwards:
        c.wait_recv()

    if fused:
        g = jnp.concatenate([gall[b] for b in range(n)], axis=-1)
    else:
        g = gs[...]
    gp[...] = shuffled(g.reshape(rows * levels, lon), order[...], ((1,), (0,))).reshape(
        rows, levels, lon)

    def start_row(r):
        sg = twice(gp[r - H] * kt[2, r])
        for q in range(groups):
            ua[r, 8 * q:8 * q + 8] = pt[r - H, 8 * q:8 * q + 8] * sg

    each_row(H, 2 * H, start_row)
    each_row(rows, rows + H, start_row)
    for pair in uhalo:
        start_halo(pair)
    each_row(2 * H, rows, start_row)

    def stepped(src, r, q):
        c0, cn, cs, ce, cw = (co[i, r] for i in range(5))
        part_of = pl.ds(8 * q, 8)
        u = src[r, part_of]
        return (c0 * u + (cn * src[r + 1, part_of] + cs * src[r - 1, part_of])
                + (ce * east(u) + cw * west_of(u)))

    def plain(src, dst, q, r):
        dst[r, 8 * q:8 * q + 8] = stepped(src, r, q)

    def unscaled(src, dst, q, r):
        dst[r, 8 * q:8 * q + 8] = stepped(src, r, q) * rs[r]

    def product(src, dst, q, r):
        t = stepped(src, r, q) * pt[r - H, 8 * q:8 * q + 8]
        t = t[:levels] + t[levels:]
        sums[r - H] = t if q == 0 else sums[r - H] + t

    chain = [ub, ud] * SWEEP
    first_sweep, second_sweep = [], []
    for k in range(SWEEP):
        last = k == SWEEP - 1
        before = chain[k - 1]
        first_sweep.append(
            (ua if k == 0 else before, uc if last else chain[k], unscaled if last else plain))
        second_sweep.append(
            (uc if k == 0 else before, None if last else chain[k], product if last else plain))

    def inner(sweep, q):
        for k, (src, dst, fn) in enumerate(sweep):
            each_row(H + k + 1, H + rows - k - 1, functools.partial(fn, src, dst, q), 8)

    def edge(sweep, q):
        for k, (src, dst, fn) in enumerate(sweep):
            for first in (k + 1, rows + H - k - 1):
                for r in range(first, first + H):
                    fn(src, dst, q, r)

    for q in range(groups):
        inner(first_sweep, q)
        if q == 0:
            wait_halo(khalo)
            for r in (*range(1, H + 1), *range(H + rows, 2 * H + rows - 1)):
                coefficient_row(r)
        wait_halo(uhalo[q])
        edge(first_sweep, q)
        start_halo(chalo[q])

    spans = ((H, rows - 2 * H), (0, H), (rows - H, H))
    pairs, pcopies = {}, []

    def pair_part(i):
        at, count = spans[i]
        t = sums[at:at + count].reshape(count * levels, lon)
        t = shuffled(t, order[...], ((1,), (1,))).reshape(count, levels, lon)
        if not fused:
            part[0, 0, at:at + count] = t
            return
        for b in range(n):
            part[b % 2, b // 2, at:at + count] = t[:, :, b * width:(b + 1) * width]
        rows_of = pl.ds(at, count)
        pairs[i] = remote(part.at[1 - core, :, rows_of], spart.at[:, rows_of],
                          psend.at[0, i], precv.at[0, i], sibling)
        pairs[i].start()

    def send_part(i):
        if not fused:
            return
        at, count = spans[i]
        rows_of = pl.ds(at, count)
        pairs[i].wait_recv()
        comb[:, at:at + count] = part[core, :, rows_of] + spart[:, at:at + count]
        for d in range(1, chips):
            c = remote(comb.at[chip_at(d), rows_of], rpart.at[d, rows_of],
                       psend.at[d, i], precv.at[d, i], 2 * chip_at(d) + core)
            c.start()
            pcopies.append(c)

    for q in range(groups):
        inner(second_sweep, q)
        if q == groups - 1:
            pair_part(0)
        wait_halo(chalo[q])
        edge(second_sweep, q)
    send_part(0)
    for i in (1, 2):
        pair_part(i)
    for i in (1, 2):
        send_part(i)

    if fused:
        for c in pcopies:
            c.wait_recv()
        acc = comb[chip]
        for d in range(1, chips):
            acc = acc + rpart[d]
        out_ref[...] = jnp.swapaxes(acc, 0, 1) / jnp.float32(total - 1)
    else:
        out_ref[...] = jnp.swapaxes(part[0, 0], 0, 1) / jnp.float32(total - 1)

    for pair in (khalo, *uhalo, *chalo):
        wait_sent(pair)
    for c in (*gcopies, *forwards, *pairs.values(), *pcopies):
        c.wait_send()


def shards(n, nz, perturb, gradient, k_north, k_east, scale):
    members, levels, rows, lon = perturb.shape
    block = gradient.shape[2]
    fused = block % 128 == 0
    if not fused:
        gradient = lax.all_gather(gradient, "mem", axis=2, tiled=True)
    width = gradient.shape[2]
    units = members * levels
    f32 = jnp.float32
    blocks, cores = (n, 2) if fused else (1, 1)
    vmem = pl.BlockSpec(memory_space=pltpu.VMEM)
    out = pl.pallas_call(
        functools.partial(sweep_kernel, n, nz, fused),
        out_shape=jax.ShapeDtypeStruct((levels, rows, width), f32),
        in_specs=[vmem] * 5,
        out_specs=vmem,
        scratch_shapes=[
            pltpu.VMEM((rows, units, lon), f32),
            pltpu.VMEM((3, rows + 2 * H, levels, lon), f32),
            pltpu.VMEM((5, rows + 2 * H, 2 * levels, lon), f32),
            pltpu.VMEM((rows + 2 * H, 2 * levels, lon), f32),
            pltpu.VMEM((rows + 2 * H, units, lon), f32),
            pltpu.VMEM((rows + 2 * H, units, lon), f32),
            pltpu.VMEM((rows + 2 * H, units, lon), f32),
            pltpu.VMEM((rows + 2 * H, units, lon), f32),
            pltpu.VMEM((lon, lon), jnp.bfloat16),
            pltpu.VMEM((rows, levels, lon), f32),
            pltpu.VMEM((rows, levels, lon), f32),
            pltpu.VMEM((rows, levels, width), f32),
            pltpu.VMEM((blocks, rows, levels, width), f32),
            pltpu.VMEM((cores, blocks // cores, rows, levels, width), f32),
            pltpu.VMEM((blocks // cores, rows, levels, width), f32),
            pltpu.VMEM((blocks // cores, rows, levels, width), f32),
            pltpu.VMEM((blocks // cores, rows, levels, width), f32),
            pltpu.SemaphoreType.DMA((2, 1)),
            pltpu.SemaphoreType.DMA((2, 1)),
            pltpu.SemaphoreType.DMA((2, members // 2)),
            pltpu.SemaphoreType.DMA((2, members // 2)),
            pltpu.SemaphoreType.DMA((2, members // 2)),
            pltpu.SemaphoreType.DMA((2, members // 2)),
            pltpu.SemaphoreType.DMA((n,)),
            pltpu.SemaphoreType.DMA((n,)),
            pltpu.SemaphoreType.DMA((n, 3)),
            pltpu.SemaphoreType.DMA((n, 3)),
        ],
        compiler_params=pltpu.CompilerParams(
            collective_id=0, has_side_effects=True, vmem_limit_bytes=48 * 1024 * 1024),
    )(perturb, gradient, k_north, k_east, scale)
    if not fused:
        out = lax.psum_scatter(out, "mem", scatter_dimension=2, tiled=True)
    return out


def solution(mesh):
    placed = (
        P("mem", None, "lat", None),
        P(None, "lat", "mem"),
        P(None, "lat", None),
        P(None, "lat", None),
        P(None, "lat", None),
    )
    return jax.shard_map(
        functools.partial(shards, mesh.shape["mem"], mesh.shape["lat"]),
        mesh=mesh, in_specs=placed, out_specs=P(None, "lat", "mem"), check_vma=False)
```

time: 41.4 us -> 40.2 us (0.971)
  Pallas kernels: 35.3 us -> 34.1 us
    pallas_call x1, Pallas kernels: 35.3 us -> 34.1 us  [shards(): pl.pallas_call(functools.partial(sweep_kernel, n, nz, fused), out_shape=j...]
where the time goes in v2:
time: 40.2 us; the launch traced here: 39.9 us
  Pallas kernels  34.1 us (85%)
  local copies, waits for them, and re-layouts  5.82 us (14%)
    pallas_call x1, Pallas kernels, shards(): pl.pallas_call(functools.partial(sweep_kernel, n, nz, fused), out_shape=j...  34.1 us
    unnamed x11, local copies, waits for them, and re-layouts  5.82 us

profile of v2, /device:TPU:0, one launch (start us, length us, event | category | flops | bytes accessed | tf_op | source)
XLA Modules:
  0.0 39.9 jit_solution(5522823067994476682)
XLA Ops:
  0.0 0.0 copy-start
  0.0 1.2 %copy-done = bf16[4,4,32,1024]{3,2,1,0:T(8,128)(2,1)S(1)} copy-done((bf16[4,4,32,1024]{3,2,1,0:T(8,128)(2,1)S(1)}, bf16[4,4,32,1024]{3,2,1,0:T(8,128)(2,1)}, u32[]{:S(2)}) %copy-start) | copy-done | bytes 1048600
  1.2 0.0 copy-start.1
  1.2 1.0 %copy-done.1 = f32[4,32,1024]{2,1,0:T(8,128)S(1)} copy-done((f32[4,32,1024]{2,1,0:T(8,128)S(1)}, f32[4,32,1024]{2,1,0:T(8,128)}, u32[]{:S(2)}) %copy-start.1) | copy-done | bytes 524312
  2.3 0.0 copy-start.2
  2.3 1.0 %copy-done.2 = f32[4,32,1024]{2,1,0:T(8,128)S(1)} copy-done((f32[4,32,1024]{2,1,0:T(8,128)S(1)}, f32[4,32,1024]{2,1,0:T(8,128)}, u32[]{:S(2)}) %copy-start.2) | copy-done | bytes 524312
  3.3 0.0 copy-start.3
  3.3 1.0 %copy-done.3 = f32[4,32,1024]{2,1,0:T(8,128)S(1)} copy-done((f32[4,32,1024]{2,1,0:T(8,128)S(1)}, f32[4,32,1024]{2,1,0:T(8,128)}, u32[]{:S(2)}) %copy-start.3) | copy-done | bytes 524312
  4.4 0.0 copy-start.4
  4.4 0.8 %copy-done.4 = f32[4,32,128]{2,1,0:T(8,128)S(1)} copy-done((f32[4,32,128]{2,1,0:T(8,128)S(1)}, f32[4,32,128]{2,1,0:T(8,128)}, u32[]{:S(2)}) %copy-start.4) | copy-done | bytes 65560
  5.2 34.1 %shard_map.55 = f32[4,32,128]{2,1,0:T(8,128)S(1)} custom-call(bf16[4,4,32,1024]{3,2,1,0:T(8,128)(2,1)S(1)} %copy-done, f32[4,32,128]{2,1,0:T(8,128)S(1)} %copy-done.4, f32[4,32,1024]{2,1,0:T(8,128)S(1)} %copy-done.1, f32[4,32,1024]{2,1,0:T(8,128)S(1)} %copy-done.2, f32[4,32,1024]{2,1,0:T(8,128)S(1)} %copy-done.3), custom_call_target="tpu_custom_call" | custom-call | tf_op jit(solution)/shard_map/pallas_call | solution.py:328
  39.3 0.6 %copy.7 = f32[4,32,128]{2,1,0:T(8,128)} copy(f32[4,32,128]{2,1,0:T(8,128)S(1)} %shard_map.55) | data formatting | bytes 131072
Async XLA Ops:
  0.0 1.2 %copy-start = (bf16[4,4,32,1024]{3,2,1,0:T(8,128)(2,1)S(1)}, bf16[4,4,32,1024]{3,2,1,0:T(8,128)(2,1)}, u32[]{:S(2)}) copy-start(bf16[4,4,32,1024]{3,2,1,0:T(8,128)(2,1)} %p_ref.1) | copy-start | bytes 3145732
  1.2 1.0 %copy-start.1 = (f32[4,32,1024]{2,1,0:T(8,128)S(1)}, f32[4,32,1024]{2,1,0:T(8,128)}, u32[]{:S(2)}) copy-start(f32[4,32,1024]{2,1,0:T(8,128)} %kn_ref.1) | copy-start | bytes 1572868
  2.3 1.0 %copy-start.2 = (f32[4,32,1024]{2,1,0:T(8,128)S(1)}, f32[4,32,1024]{2,1,0:T(8,128)}, u32[]{:S(2)}) copy-start(f32[4,32,1024]{2,1,0:T(8,128)} %ke_ref.1) | copy-start | bytes 1572868
  3.3 1.0 %copy-start.3 = (f32[4,32,1024]{2,1,0:T(8,128)S(1)}, f32[4,32,1024]{2,1,0:T(8,128)}, u32[]{:S(2)}) copy-start(f32[4,32,1024]{2,1,0:T(8,128)} %s_ref.1) | copy-start | bytes 1572868
  4.4 0.8 %copy-start.4 = (f32[4,32,128]{2,1,0:T(8,128)S(1)}, f32[4,32,128]{2,1,0:T(8,128)}, u32[]{:S(2)}) copy-start(f32[4,32,128]{2,1,0:T(8,128)} %g_ref.1) | copy-start | bytes 196612
